TPU v7x, 32 devices: a whole 2x2x4 slice. The times are simulated.
32 devices in a mesh: row: 8 (over z, core), col: 4 (over y, x).
Axes of the slice: x: 2, y: 2, z: 4, core: 2. Of those that a mesh axis runs over, the one named last changes fastest.
Arguments:
- momentum: bfloat16 [12288, 26624], P('row', 'col'), may hold values from -13 to 13
- gradient: bfloat16 [12288, 26624], P('row', 'col'), may hold values from -0.59765625 to 0.59765625
- basis: float32 [256, 26624], P('row', 'col'), may hold values from -0.0390625 to 0.0390625
Outputs:
- momentum_new: bfloat16 [12288, 26624], P('row', 'col')
- basis_new: float32 [256, 26624], P('row', 'col')
- left_factor: float32 [12288, 256], P(('row', 'col'))
All inputs are finite; a program needn't handle non-finite values.
Results may differ from a plain program's by a relative error of at most 0.0073.
The roundings to bfloat16 on the way count: a program that leaves them out, or rounds other values in their place, can miss the bound.
Values may be sent and summed in bfloat16 or wider, within the bound.
A program may use at most 192 MiB of HBM per device.

v0:
```python
import jax
import jax.numpy as jnp
from jax import lax
from jax.sharding import PartitionSpec as P

COLS = 26624
POWER = 2


decay_rate = 0.95
epsilon = 1e-06


def per_device(momentum, gradient, basis):
    buffer = (momentum.astype(jnp.float32) + gradient.astype(jnp.float32)).astype(jnp.bfloat16)
    block_rows = buffer.shape[0]
    share = block_rows // lax.axis_size("col")
    col_index = lax.axis_index("col")
    directions = basis.astype(jnp.bfloat16)
    for step in range(POWER):
        partial_value = lax.dot_general(
            buffer,
            lax.all_gather(directions, "row", axis=0, tiled=True),
            (((1,), (1,)), ((), ())),
            preferred_element_type=jnp.float32,
        )
        power = lax.psum(partial_value, "col")
        gram = lax.psum(jnp.dot(power.T, power, precision=lax.Precision.HIGHEST), "row")
        chol = jnp.linalg.cholesky(gram)
        left_full = lax.linalg.triangular_solve(
            chol, power, left_side=False, lower=True, transpose_a=True
        )
        left_share = lax.dynamic_slice_in_dim(left_full, col_index * share, share, 0)
        left_half = left_full.astype(jnp.bfloat16)

        def right_term():
            return lax.dot_general(
                left_half, buffer, (((0,), (0,)), ((), ())), preferred_element_type=jnp.float32
            )

        if step + 1 < POWER:
            right_own = lax.psum_scatter(right_term(), "row", scatter_dimension=0, tiled=True)
            directions = right_own.astype(jnp.bfloat16)
    right_own = lax.psum_scatter(right_term(), "row", scatter_dimension=0, tiled=True)
    squares = lax.psum(jnp.sum(right_own * right_own, axis=1), "col")
    right_whole = lax.all_gather(right_own.astype(jnp.bfloat16), "row", axis=0, tiled=True)
    basis_new = right_own / jnp.sqrt(squares[:, None] / COLS + epsilon)
    update = jnp.dot(left_half, right_whole, preferred_element_type=jnp.float32)
    momentum_new = (buffer.astype(jnp.float32) - (1.0 - decay_rate) * update).astype(jnp.bfloat16)
    return (momentum_new, basis_new, left_share)


def solution(mesh):
    return jax.shard_map(
        per_device,
        mesh=mesh,
        in_specs=(P("row", "col"), P("row", "col"), P("row", "col")),
        out_specs=(P("row", "col"), P("row", "col"), P(("row", "col"), None)),
        check_vma=False,
    )
```

profile of v0, /device:TPU:0, one launch (start us, length us, event | category | flops | bytes accessed | tf_op | source)
XLA Modules:
  0.0 741.5 jit_solution(9893952512805365480)
XLA Ops:
  7.2 2.0 convert_element_type.34
  9.2 22.4 %add_convert_fusion = bf16[1536,6656]{1,0:T(8,128)(2,1)} fusion(bf16[1536,6656]{1,0:T(8,128)(2,1)} %param.7, bf16[1536,6656]{1,0:T(8,128)(2,1)} %param.6), kind=kLoop, calls=%fused_computation.5 | loop fusion | flops 40894464 | bytes 61341696 | tf_op jit(solution)/shard_map/convert_element_type | solution.py:15
  31.6 21.7 %all-gather.4.cloned.1.call-done = bf16[256,6656]{1,0:T(8,128)(2,1)} async-done(((bf16[32,6656]{1,0:T(8,128)(2,1)}), bf16[256,6656]{1,0:T(8,128)(2,1)}) %all-gather.4.cloned.1.call-update) | async-done | bytes 3407888 | tf_op jit(solution)/shard_map/all_gather | solution.py:23
  53.4 11.5 %fusion.31 = f32[1536,256]{1,0:T(8,128)} fusion(bf16[1536,6656]{1,0:T(8,128)(2,1)} %add_convert_fusion, bf16[256,6656]{1,0:T(8,128)(2,1)} %all-gather.4.cloned.1.call-done), kind=kOutput, calls=%fused_computation.70 | convolution fusion | flops 5234491392 | bytes 25427968 | tf_op jit(solution)/shard_map/dot_general | solution.py:21
  64.9 59.9 %all-reduce.6.cloned.1.call-done = f32[1536,256]{1,0:T(8,128)} async-done(((f32[1536,256]{1,0:T(8,128)}), f32[1536,256]{1,0:T(8,128)}) %all-reduce.6.cloned.1.call-update) | async-done | bytes 1572880 | tf_op jit(solution)/shard_map/psum | solution.py:27
  124.8 5.3 fusion.32
  130.2 0.5 reduce-scatter.3.cloned.1.call-start
  130.7 54.6 %all-reduce.8.cloned.1.call-done = f32[256,256]{0,1:T(8,128)} async-done(((f32[256,256]{0,1:T(8,128)}), f32[256,256]{0,1:T(8,128)}) %all-reduce.8.cloned.1.call-update) | async-done | bytes 262160 | tf_op jit(solution)/shard_map/psum | solution.py:28
  185.3 1.1 copy.7
  186.4 1.0 fusion.8
  187.4 11.7 %cholesky.130 = f32[128,128]{1,0:T(8,128)S(1)} custom-call(f32[128,128]{1,0:T(8,128)S(1)} %cholesky.194), custom_call_target="Cholesky" | custom-call | tf_op jit(solution)/shard_map/jit(cholesky)/cholesky | solution.py:29
  199.1 9.8 %custom-call.13 = f32[1,128,128]{1,2,0:T(8,128)S(1)} custom-call(f32[1,128,128]{2,1,0:T(8,128)S(1)} %get-tuple-element.53), custom_call_target="InvertDiagBlocksLowerTriangular" | custom-call | tf_op jit(solution)/shard_map/jit(cholesky)/cholesky | solution.py:29
  208.9 0.2 constant_dynamic-update-slice_fusion.3
  209.2 0.3 convolution_subtract_fusion.3
  209.4 11.7 %cholesky.147 = f32[128,128]{1,0:T(8,128)S(1)} custom-call(f32[128,128]{1,0:T(8,128)S(1)} %convolution_subtract_fusion.3), custom_call_target="Cholesky" | custom-call | tf_op jit(solution)/shard_map/jit(cholesky)/cholesky | solution.py:29
  221.2 0.7 compare_reduce_fusion.2
  223.1 0.1 broadcast.93
  223.2 4.1 while.4
  223.4 0.6 fusion.56
  224.0 1.3 bitcast_dynamic-update-slice_fusion.4
  225.4 0.6 fusion.56
  226.0 1.3 bitcast_dynamic-update-slice_fusion.4
  227.3 19.7 %custom-call.14 = f32[2,128,128]{1,2,0:T(8,128)S(1)} custom-call(f32[2,128,128]{2,1,0:T(8,128)S(1)} %get-tuple-element.19), custom_call_target="InvertDiagBlocksLowerTriangular" | custom-call | tf_op jit(solution)/shard_map/triangular_solve/custom-call.0 | solution.py:30
  247.0 0.9 fusion.4
  247.9 1.4 convolution_subtract_fusion.1
  249.3 0.9 fusion.16
  250.2 14.4 %fusion.1 = f32[256,6656]{1,0:T(8,128)} fusion(bf16[1536,6656]{1,0:T(8,128)(2,1)} %add_convert_fusion, bf16[1536,128]{0,1:T(8,128)(2,1)S(1)} %fusion.16, f32[1536,128]{0,1:T(8,128)S(1)} %bitcast.78), kind=kOutput, calls=%fused_computation.16 | convolution fusion | flops 5236064256 | bytes 28442624 | tf_op jit(solution)/shard_map/dot_general | solution.py:37
  264.7 0.0 all-gather.6.cloned.1.call-start
  264.7 73.9 %reduce-scatter.3.cloned.1.call-done = f32[32,6656]{1,0:T(8,128)} async-done(((f32[256,6656]{1,0:T(8,128)}), f32[32,6656]{1,0:T(8,128)}) %reduce-scatter.3.cloned.1.call-update) | async-done | bytes 851984 | tf_op jit(solution)/shard_map/reduce_scatter | solution.py:42
  338.6 2.0 convert_element_type.36
  340.6 38.9 %all-gather.6.cloned.1.call-done = bf16[256,6656]{1,0:T(8,128)(2,1)} async-done(((bf16[32,6656]{1,0:T(8,128)(2,1)}), bf16[256,6656]{1,0:T(8,128)(2,1)}) %all-gather.6.cloned.1.call-update) | async-done | bytes 3407888 | tf_op jit(solution)/shard_map/all_gather | solution.py:23
  379.5 11.5 %fusion.33 = f32[1536,256]{1,0:T(8,128)} fusion(bf16[1536,6656]{1,0:T(8,128)(2,1)} %add_convert_fusion, bf16[256,6656]{1,0:T(8,128)(2,1)} %all-gather.6.cloned.1.call-done), kind=kOutput, calls=%fused_computation.72 | convolution fusion | flops 5234491392 | bytes 25427968 | tf_op jit(solution)/shard_map/dot_general | solution.py:21
  391.0 0.0 all-reduce.12.cloned.1.call-start
  391.0 59.8 %all-reduce.10.cloned.1.call-done = f32[1536,256]{1,0:T(8,128)} async-done(((f32[1536,256]{1,0:T(8,128)}), f32[1536,256]{1,0:T(8,128)}) %all-reduce.10.cloned.1.call-update) | async-done | bytes 1572880 | tf_op jit(solution)/shard_map/psum | solution.py:27
  450.9 5.3 fusion.34
  456.3 0.3 reduce-scatter.5.cloned.1.call-start
  456.5 54.8 %all-reduce.12.cloned.1.call-done = f32[256,256]{0,1:T(8,128)} async-done(((f32[256,256]{0,1:T(8,128)}), f32[256,256]{0,1:T(8,128)}) %all-reduce.12.cloned.1.call-update) | async-done | bytes 262160 | tf_op jit(solution)/shard_map/psum | solution.py:28
  511.3 1.1 copy.9
  512.4 1.0 fusion.7
  513.4 11.7 %cholesky.164 = f32[128,128]{1,0:T(8,128)S(1)} custom-call(f32[128,128]{1,0:T(8,128)S(1)} %cholesky.197), custom_call_target="Cholesky" | custom-call | tf_op jit(solution)/shard_map/jit(cholesky)/cholesky | solution.py:29
  525.2 9.8 %custom-call.15 = f32[1,128,128]{1,2,0:T(8,128)S(1)} custom-call(f32[1,128,128]{2,1,0:T(8,128)S(1)} %get-tuple-element.49), custom_call_target="InvertDiagBlocksLowerTriangular" | custom-call | tf_op jit(solution)/shard_map/jit(cholesky)/cholesky | solution.py:29
  535.0 0.2 constant_dynamic-update-slice_fusion.1
  535.2 0.3 convolution_subtract_fusion.2
  535.5 11.7 %cholesky.181 = f32[128,128]{1,0:T(8,128)S(1)} custom-call(f32[128,128]{1,0:T(8,128)S(1)} %convolution_subtract_fusion.2), custom_call_target="Cholesky" | custom-call | tf_op jit(solution)/shard_map/jit(cholesky)/cholesky | solution.py:29
  547.2 0.6 compare_reduce_fusion.1
  547.9 0.7 compare_reduce_fusion
  549.9 4.2 while.5
  550.1 0.6 fusion.57
  550.7 1.3 bitcast_dynamic-update-slice_fusion.5
  552.1 0.6 fusion.57
  552.7 1.3 bitcast_dynamic-update-slice_fusion.5
  554.0 19.7 %custom-call.16 = f32[2,128,128]{1,2,0:T(8,128)S(1)} custom-call(f32[2,128,128]{2,1,0:T(8,128)S(1)} %get-tuple-element.20), custom_call_target="InvertDiagBlocksLowerTriangular" | custom-call | tf_op jit(solution)/shard_map/triangular_solve/custom-call.0 | solution.py:30
  573.7 0.9 fusion.2
  574.6 1.4 convolution_subtract_fusion
  576.0 0.8 fusion.12
  576.9 14.3 %fusion.10 = f32[256,6656]{1,0:T(8,128)} fusion(bf16[1536,6656]{1,0:T(8,128)(2,1)} %add_convert_fusion, f32[1536,128]{0,1:T(8,128)S(1)} %fusion.12, f32[1536,128]{0,1:T(8,128)S(1)} %bitcast.75), kind=kOutput, calls=%fused_computation.30 | convolution fusion | flops 5236064256 | bytes 28835840 | tf_op jit(solution)/shard_map/dot_general | solution.py:37
  591.2 0.0 all-gather.8.cloned.1.call-start
  591.3 73.9 %reduce-scatter.5.cloned.1.call-done = f32[32,6656]{1,0:T(8,128)} async-done(((f32[256,6656]{1,0:T(8,128)}), f32[32,6656]{1,0:T(8,128)}) %reduce-scatter.5.cloned.1.call-update) | async-done | bytes 851984 | tf_op jit(solution)/shard_map/reduce_scatter | solution.py:44
  665.1 1.3 multiply_reduce_fusion
  666.4 9.8 %psum.39 = f32[32]{0:T(128)S(1)} all-reduce(f32[32]{0:T(128)S(1)} %multiply_reduce_fusion), channel_id=1, replica_groups=mesh['row'=8,'col'=4] {'col'}, use_global_device_ids=true, to_apply=%region_11.14 | all-reduce | flops 32 | bytes 256 | tf_op jit(solution)/shard_map/psum | solution.py:45
  676.3 2.7 broadcast_divide_fusion
  679.1 0.9 copy.10
  680.0 36.2 %all-gather.8.cloned.1.call-done = bf16[256,6656]{1,0:T(8,128)(2,1)} async-done(((bf16[32,6656]{1,0:T(8,128)(2,1)}), bf16[256,6656]{1,0:T(8,128)(2,1)}) %all-gather.8.cloned.1.call-update) | async-done | bytes 3407888 | tf_op jit(solution)/shard_map/all_gather | solution.py:46
  716.2 18.3 %subtract_convert_fusion = bf16[1536,6656]{1,0:T(8,128)(2,1)} fusion(bf16[1536,6656]{1,0:T(8,128)(2,1)} %add_convert_fusion, bf16[256,6656]{1,0:T(8,128)(2,1)} %all-gather.8.cloned.1.call-done, f32[1536,128]{0,1:T(8,128)S(1)} %fusion.12, f32[1536,128]{0,1:T(8,128)S(1)} %bitcast.77), kind=kOutput, calls=%fused_computation.4 | convolution fusion | flops 5276958720 | bytes 45875200 | tf_op jit(solution)/shard_map/dot_general | solution.py:48
  (36 shorter events, 0.7 us)
Async XLA Ops:
  7.2 46.2 %all-gather.4.cloned.1.call-start = ((), (), s32[]{:S(2)}) async-start(), calls=%async_computation.2 | async-start | bytes 3833856 | tf_op jit(solution)/shard_map/all_gather | solution.py:23
  9.2 115.6 %all-reduce.6.cloned.1.call-start = ((), (), s32[]{:S(2)}) async-start(), calls=%async_computation.3 | async-start | bytes 3145728 | tf_op jit(solution)/shard_map/psum | solution.py:27
  64.9 120.4 %all-reduce.8.cloned.1.call-start = ((), (), s32[]{:S(2)}) async-start(), calls=%async_computation.4 | async-start | bytes 524288 | tf_op jit(solution)/shard_map/psum | solution.py:28
  124.8 122.2 %copy-start = (f32[1536,256]{1,0:T(8,128)S(1)}, f32[1536,256]{1,0:T(8,128)}, u32[]{:S(2)}) copy-start(f32[1536,256]{1,0:T(8,128)} %all-reduce.6.cloned.1.call-done) | copy-start | bytes 4718596
  130.2 208.4 %reduce-scatter.3.cloned.1.call-start = ((), (), s32[]{:S(2)}) async-start(), calls=%async_computation.5 | async-start | bytes 7667712 | tf_op jit(solution)/shard_map/reduce_scatter | solution.py:42
  264.7 114.8 %all-gather.6.cloned.1.call-start = ((), (), s32[]{:S(2)}) async-start(), calls=%async_computation.6 | async-start | bytes 3833856 | tf_op jit(solution)/shard_map/all_gather | solution.py:23
  340.5 110.3 %all-reduce.10.cloned.1.call-start = ((), (), s32[]{:S(2)}) async-start(), calls=%async_computation.7 | async-start | bytes 3145728 | tf_op jit(solution)/shard_map/psum | solution.py:27
  391.0 120.3 %all-reduce.12.cloned.1.call-start = ((), (), s32[]{:S(2)}) async-start(), calls=%async_computation.8 | async-start | bytes 524288 | tf_op jit(solution)/shard_map/psum | solution.py:28
  450.9 122.8 %copy-start.1 = (f32[1536,256]{1,0:T(8,128)S(1)}, f32[1536,256]{1,0:T(8,128)}, u32[]{:S(2)}) copy-start(f32[1536,256]{1,0:T(8,128)} %all-reduce.10.cloned.1.call-done) | copy-start | bytes 4718596
  456.3 208.9 %reduce-scatter.5.cloned.1.call-start = ((), (), s32[]{:S(2)}) async-start(), calls=%async_computation.9 | async-start | bytes 7667712 | tf_op jit(solution)/shard_map/reduce_scatter | solution.py:44
  591.2 125.0 %all-gather.8.cloned.1.call-start = ((), (), s32[]{:S(2)}) async-start(), calls=%async_computation.10 | async-start | bytes 3833856 | tf_op jit(solution)/shard_map/all_gather | solution.py:46
Sparse Core Ops, SparseCore 0:
  10.2 43.1 all-gather.3
  65.0 59.7 all-reduce.5
  130.3 54.9 all-reduce.7
  264.8 73.7 reduce-scatter.2
  340.7 38.7 all-gather.5
  391.1 59.7 all-reduce.9
  456.4 54.9 all-reduce.11
  591.3 73.7 reduce-scatter.4
  679.2 36.9 all-gather.7
where the time goes:
time: 746 us; the launch traced here: 741 us
  waiting for transfers between devices  474 us (64%)
  other arithmetic  140 us (19%)
  matrix products  88 us (12%)
  between operations  17 us (2%)
  local copies, waits for them, and re-layouts  11 us (1%)
  blocking collectives  9.85 us (1%)
    reduce_scatter x2, waiting for transfers between devices, per_device(): lax.psum_scatter(right_term(), 'row', scatter_dimension=0, tiled=True)  148 us
    psum x2, waiting for transfers between devices, per_device(): power = lax.psum(partial_value, 'col')  120 us
    psum x2, waiting for transfers between devices, per_device(): lax.psum(jnp.dot(power.T, power, precision=lax.Precision.HIGHEST), 'row')  109 us
    another operation x13, other arithmetic, per_device(): chol = jnp.linalg.cholesky(gram)  68.6 us
    all_gather x2, waiting for transfers between devices, per_device(): lax.all_gather(directions, 'row', axis=0, tiled=True)  60.6 us
    another operation x6, other arithmetic, per_device(): lax.linalg.triangular_solve(chol, power, left_side=False, lower=True, tra...  39.5 us
    all_gather x1, waiting for transfers between devices, per_device(): lax.all_gather(right_own.astype(jnp.bfloat16), 'row', axis=0, tiled=True)  36.2 us
    dot_general x2, matrix products, right_term(): lax.dot_general(left_half, buffer, (((0,), (0,)), ((), ())), preferred_el...  28.8 us
  transfers between devices with their start and end apart: 9, of which 9 were waited for; matrix products, arithmetic and copies ran while one was open for 3% of the time, Pallas kernels for 0%

commit v1 on v0

v1 whole, which is shorter than its diff:
```python
import functools

import jax
import jax.numpy as jnp
from jax import lax
from jax.experimental import pallas as pl
from jax.experimental.pallas import tpu as pltpu
from jax.sharding import PartitionSpec as P

COLS = 26624
POWER = 2
BLOCK = 128
PANEL = 8
MESH = pl.DeviceIdType.MESH
HIGHEST = lax.Precision.HIGHEST


decay_rate = 0.95
epsilon = 1e-06


def dot(a, b, ca, cb, precision=HIGHEST):
    return lax.dot_general(
        a, b, (((ca,), (cb,)), ((), ())), precision=precision, preferred_element_type=jnp.float32
    )


def inverse_factor(a, work, inv):
    n = BLOCK
    work[...] = a
    rows = lax.broadcasted_iota(jnp.int32, (n, n), 0)
    lanes = lax.broadcasted_iota(jnp.int32, (n, n), 1)
    inv[...] = jnp.where(rows == lanes, 1.0, 0.0).astype(jnp.float32)
    sub = lax.broadcasted_iota(jnp.int32, (PANEL, n), 0)
    lane = lax.broadcasted_iota(jnp.int32, (PANEL, n), 1)

    def panel(p, carry):
        at = pl.multiple_of(p * PANEL, PANEL)
        pa = work[pl.ds(at, PANEL), :]
        pm = inv[pl.ds(at, PANEL), :]
        d = pltpu.roll(pa, n - at, 1)
        for k in range(PANEL):
            pivot = jnp.broadcast_to(d[k : k + 1, k : k + 1], (PANEL, n))
            r = lax.rsqrt(pivot)
            r = r * (1.5 - 0.5 * (pivot * r) * r)
            column = jnp.broadcast_to(d[:, k : k + 1], (PANEL, n)) * r
            dk = jnp.broadcast_to(d[k : k + 1, :], (PANEL, n)) * r
            ak = jnp.broadcast_to(pa[k : k + 1, :], (PANEL, n)) * r
            mk = jnp.broadcast_to(pm[k : k + 1, :], (PANEL, n)) * r
            below = sub > k
            here = sub == k
            d = jnp.where(here, dk, jnp.where(below, d - column * dk, d))
            pa = jnp.where(here, ak, jnp.where(below, pa - column * ak, pa))
            pm = jnp.where(here, mk, jnp.where(below, pm - column * mk, pm))
        inv[pl.ds(at, PANEL), :] = pm
        lhs = jnp.where(lane >= at + PANEL, pa, 0.0)
        work[...] -= dot(lhs, pa, 0, 0)
        inv[...] -= dot(lhs, pm, 0, 0)
        return carry

    lax.fori_loop(0, n // PANEL, panel, 0)


def left_kernel(
    n_row, n_col, gather, p_ref, left_ref, *rest
):
    if gather:
        half_ref, *rest = rest
    (recv_p, own_p, gpart, recv_g, gown, recv_c, gfull, work, inv1, inv2, half_own,
     sp, rp, sg, rg, sc, rc, sa, ra, sh, rh) = rest
    row, col = lax.axis_index("row"), lax.axis_index("col")
    share = left_ref.shape[0]
    gr = gown.shape[0]
    rank = gfull.shape[0]

    def row_peer(d):
        return lax.rem(row + d, n_row)

    def col_peer(d):
        return lax.rem(col + d, n_col)

    barrier = pltpu.get_barrier_semaphore()
    for d in range(1, n_row):
        pl.semaphore_signal(barrier, inc=1, device_id=(row_peer(d), col), device_id_type=MESH)
    for d in range(1, n_col):
        pl.semaphore_signal(barrier, inc=1, device_id=(row, col_peer(d)), device_id_type=MESH)
    pl.semaphore_wait(barrier, n_row + n_col - 2)

    def remote(src, dst, send, recv, peer):
        c = pltpu.make_async_remote_copy(
            src_ref=src, dst_ref=dst, send_sem=send, recv_sem=recv,
            device_id=peer, device_id_type=MESH,
        )
        c.start()
        return c

    copies = []
    for d in range(1, n_col):
        peer = col_peer(d)
        at = pl.multiple_of(peer * share, 8)
        copies.append(remote(p_ref.at[pl.ds(at, share)], recv_p.at[d - 1], sp.at[d - 1], rp.at[d - 1], (row, peer)))
    total = p_ref[pl.ds(pl.multiple_of(col * share, 8), share), :]
    for d in range(1, n_col):
        copies[d - 1].wait()
        total = total + recv_p[d - 1]
    own_p[...] = total

    gpart[...] = dot(own_p[...], own_p[...], 0, 0)
    copies = []
    for d in range(1, n_row):
        peer = row_peer(d)
        at = pl.multiple_of(peer * gr, 8)
        copies.append(remote(gpart.at[pl.ds(at, gr)], recv_g.at[d - 1], sg.at[d - 1], rg.at[d - 1], (peer, col)))
    mine = pl.multiple_of(row * gr, 8)
    total = gpart[pl.ds(mine, gr), :]
    for d in range(1, n_row):
        copies[d - 1].wait()
        total = total + recv_g[d - 1]
    recv_c[pl.ds(col, 1)] = total[None]
    copies = []
    for d in range(1, n_col):
        copies.append(remote(recv_c.at[col], recv_c.at[col], sc.at[d - 1], rc.at[d - 1], (row, col_peer(d))))
    for c in copies:
        c.wait()
    total = recv_c[0]
    for i in range(1, n_col):
        total = total + recv_c[i]
    gown[...] = total
    gfull[pl.ds(mine, gr), :] = total
    copies = []
    for d in range(1, n_row):
        copies.append(remote(gown, gfull.at[pl.ds(mine, gr)], sa.at[d - 1], ra.at[d - 1], (row_peer(d), col)))
    for c in copies:
        c.wait()

    b = BLOCK
    inverse_factor(gfull[:b, :b], work, inv1)
    l21 = dot(gfull[b:, :b], inv1[...], 1, 1)
    left1 = dot(own_p[:, :b], inv1[...], 1, 1)
    left_ref[:, :b] = left1
    own_p[:, b:] -= dot(left1, l21, 1, 1)
    inverse_factor(gfull[b:, b:] - dot(l21, l21, 1, 1), work, inv2)
    left_ref[:, b:] = dot(own_p[:, b:], inv2[...], 1, 1)
    if gather:
        half = left_ref[...].astype(jnp.bfloat16)
        half_own[...] = half
        at = pl.multiple_of(col * share, 16)
        half_ref[pl.ds(at, share), :] = half
        copies = []
        for d in range(1, n_col):
            copies.append(remote(half_own, half_ref.at[pl.ds(at, share)], sh.at[d - 1], rh.at[d - 1], (row, col_peer(d))))
        for c in copies:
            c.wait()


def left_of(partial, n_row, n_col):
    rows, rank = partial.shape
    share = rows // n_col
    gr = rank // n_row
    gather = share % 16 == 0
    f32 = jnp.float32
    out = [jax.ShapeDtypeStruct((share, rank), f32)]
    if gather:
        out.append(jax.ShapeDtypeStruct((rows, rank), jnp.bfloat16))
    vmem = pl.BlockSpec(memory_space=pltpu.VMEM)
    dma = pltpu.SemaphoreType.DMA
    res = pl.pallas_call(
        functools.partial(left_kernel, n_row, n_col, gather),
        out_shape=out,
        in_specs=[vmem],
        out_specs=[vmem] * len(out),
        scratch_shapes=[
            pltpu.VMEM((n_col - 1, share, rank), f32),
            pltpu.VMEM((share, rank), f32),
            pltpu.VMEM((rank, rank), f32),
            pltpu.VMEM((n_row - 1, gr, rank), f32),
            pltpu.VMEM((gr, rank), f32),
            pltpu.VMEM((n_col, gr, rank), f32),
            pltpu.VMEM((rank, rank), f32),
            pltpu.VMEM((BLOCK, BLOCK), f32),
            pltpu.VMEM((BLOCK, BLOCK), f32),
            pltpu.VMEM((BLOCK, BLOCK), f32),
            pltpu.VMEM((share, rank), jnp.bfloat16),
            dma((n_col - 1,)), dma((n_col - 1,)),
            dma((n_row - 1,)), dma((n_row - 1,)),
            dma((n_col - 1,)), dma((n_col - 1,)),
            dma((n_row - 1,)), dma((n_row - 1,)),
            dma((n_col - 1,)), dma((n_col - 1,)),
        ],
        compiler_params=pltpu.CompilerParams(
            collective_id=0, has_side_effects=True, vmem_limit_bytes=24 * 1024 * 1024
        ),
    )(partial)
    if gather:
        return res
    left = res[0]
    return left, lax.all_gather(left.astype(jnp.bfloat16), "col", axis=0, tiled=True)


def per_device(n_row, n_col, momentum, gradient, basis):
    buffer = (momentum.astype(jnp.float32) + gradient.astype(jnp.float32)).astype(jnp.bfloat16)
    directions = basis.astype(jnp.bfloat16)
    for step in range(POWER):
        partial_value = lax.dot_general(
            buffer,
            lax.all_gather(directions, "row", axis=0, tiled=True),
            (((1,), (1,)), ((), ())),
            preferred_element_type=jnp.float32,
        )
        left_share, left_half = left_of(partial_value, n_row, n_col)
        right_own = lax.psum_scatter(
            lax.dot_general(
                left_half, buffer, (((0,), (0,)), ((), ())), preferred_element_type=jnp.float32
            ),
            "row", scatter_dimension=0, tiled=True,
        )
        directions = right_own.astype(jnp.bfloat16)
    squares = lax.psum(jnp.sum(right_own * right_own, axis=1), "col")
    right_whole = lax.all_gather(directions, "row", axis=0, tiled=True)
    basis_new = right_own / jnp.sqrt(squares[:, None] / COLS + epsilon)
    update = jnp.dot(left_half, right_whole, preferred_element_type=jnp.float32)
    momentum_new = (buffer.astype(jnp.float32) - (1.0 - decay_rate) * update).astype(jnp.bfloat16)
    return (momentum_new, basis_new, left_share)


def solution(mesh):
    return jax.shard_map(
        functools.partial(per_device, mesh.shape["row"], mesh.shape["col"]),
        mesh=mesh,
        in_specs=(P("row", "col"), P("row", "col"), P("row", "col")),
        out_specs=(P("row", "col"), P("row", "col"), P(("row", "col"), None)),
        check_vma=False,
    )
```

time: 746 us -> 550 us (0.74)
  waiting for transfers between devices: 474 us -> 250 us
  Pallas kernels: 0 us -> 181 us
  other arithmetic: 140 us -> 30.3 us
  matrix products: 88 us -> 63.3 us
  local copies, waits for them, and re-layouts: 11 us -> 0.75 us
    psum x4 -> x0, waiting for transfers between devices: 229 us -> none  [the longest x2 120 us: per_device(): power = lax.psum(partial_value, 'col')]
    pallas_call x0 -> x2, Pallas kernels: none -> 181 us  [left_of(): pl.pallas_call(functools.partial(left_kernel, n_row, n_col, gather), out_...]
    another operation x19 -> x0, other arithmetic: 108 us -> none  [the longest x13 68.6 us: per_device(): chol = jnp.linalg.cholesky(gram)]
    dot_general x4 -> x2, matrix products: 39.5 us -> 22.4 us  [per_device(): lax.dot_general(left_half, buffer, (((0,), (0,)), ((), ())), preferred_el...]
    another operation x19 -> x0, local copies, waits for them, and re-layouts: 7.88 us -> none  [the longest x15 7.83 us: per_device(): lax.linalg.triangular_solve(chol, power, left_side=False, lower=True, tra...]
  transfers between devices with their start and end apart: 9 -> 5, of which waited for: 9 -> 5; matrix products, arithmetic and copies ran while one was open for 3% -> 4% of each run, Pallas kernels for 0% -> 0%
where the time goes in v1:
time: 550 us; the launch traced here: 549 us
  waiting for transfers between devices  250 us (45%)
  Pallas kernels  181 us (33%)
  matrix products  63.3 us (12%)
  other arithmetic  30.3 us (6%)
  between operations  13.8 us (3%)
  blocking collectives  9.83 us (2%)
    pallas_call x2, Pallas kernels, left_of(): pl.pallas_call(functools.partial(left_kernel, n_row, n_col, gather), out_...  181 us
    reduce_scatter x2, waiting for transfers between devices, per_device(): lax.psum_scatter(lax.dot_general(left_half, buffer, (((0,), (0,)), ((), (...  152 us
    all_gather x2, waiting for transfers between devices, per_device(): lax.all_gather(directions, 'row', axis=0, tiled=True)  60.6 us
    all_gather x1, waiting for transfers between devices, per_device(): right_whole = lax.all_gather(directions, 'row', axis=0, tiled=True)  37.1 us
    dot_general x2, matrix products, per_device(): lax.dot_general(buffer, lax.all_gather(directions, 'row', axis=0, tiled=T...  22.6 us
    convert_element_type x1, other arithmetic, per_device(): (momentum.astype(jnp.float32) + gradient.astype(jnp.float32)).astype(jnp....  22.4 us
    dot_general x2, matrix products, per_device(): lax.dot_general(left_half, buffer, (((0,), (0,)), ((), ())), preferred_el...  22.4 us
    dot_general x1, matrix products, per_device(): update = jnp.dot(left_half, right_whole, preferred_element_type=jnp.float32)  18.3 us
  transfers between devices with their start and end apart: 5, of which 5 were waited for; matrix products, arithmetic and copies ran while one was open for 4% of the time, Pallas kernels for 0%

profile of v1, /device:TPU:0, one launch (start us, length us, event | category | flops | bytes accessed | tf_op | source)
XLA Modules:
  0.0 549.3 jit_solution(3372817613343019168)
XLA Ops:
  7.2 0.0 all-gather.4.cloned.1.call-start
  7.2 2.0 convert_element_type.28
  9.2 0.0 all-gather.4.cloned.1.call-update
  9.2 0.0 reduce-scatter.3.cloned.1.call-start
  9.2 22.4 %add_convert_fusion = bf16[1536,6656]{1,0:T(8,128)(2,1)} fusion(bf16[1536,6656]{1,0:T(8,128)(2,1)} %param.4, bf16[1536,6656]{1,0:T(8,128)(2,1)} %param.3), kind=kLoop, calls=%fused_computation.1 | loop fusion | flops 40894464 | bytes 61341696 | tf_op jit(solution)/shard_map/convert_element_type | solution.py:201
  31.6 21.7 %all-gather.4.cloned.1.call-done = bf16[256,6656]{1,0:T(8,128)(2,1)} async-done(((bf16[32,6656]{1,0:T(8,128)(2,1)}), bf16[256,6656]{1,0:T(8,128)(2,1)}) %all-gather.4.cloned.1.call-update) | async-done | bytes 3407888 | tf_op jit(solution)/shard_map/all_gather | solution.py:206
  53.4 0.0 copy-start
  53.4 12.0 %fusion.p_ref = f32[1536,256]{1,0:T(8,128)S(1)} fusion(bf16[1536,6656]{1,0:T(8,128)(2,1)} %add_convert_fusion, bf16[256,6656]{1,0:T(8,128)(2,1)} %all-gather.4.cloned.1.call-done), kind=kOutput, calls=%fused_computation.5 | convolution fusion | flops 5234491392 | bytes 25427968 | tf_op jit(solution)/shard_map/dot_general | solution.py:204
  65.4 91.0 %shard_map.58 = (f32[384,256]{1,0:T(8,128)}, bf16[1536,256]{1,0:T(8,128)(2,1)S(1)}) custom-call(f32[1536,256]{1,0:T(8,128)S(1)} %fusion.p_ref), custom_call_target="tpu_custom_call" | custom-call | tf_op jit(solution)/shard_map/pallas_call | solution.py:167
  156.4 0.0 copy-done
  156.4 7.7 %fusion.1 = f32[256,6656]{1,0:T(8,128)} fusion(bf16[1536,256]{1,0:T(8,128)(2,1)S(1)} %get-tuple-element.6, bf16[1536,6656]{1,0:T(8,128)(2,1)S(1)} %copy-done), kind=kOutput, calls=%fused_computation.6 | convolution fusion | flops 5234491392 | bytes 28049408 | tf_op jit(solution)/shard_map/dot_general | solution.py:212
  164.1 0.0 reduce-scatter.3.cloned.1.call-update
  164.2 0.0 all-gather.6.cloned.1.call-start
  164.2 75.9 %reduce-scatter.3.cloned.1.call-done = f32[32,6656]{1,0:T(8,128)} async-done(((f32[256,6656]{1,0:T(8,128)}), f32[32,6656]{1,0:T(8,128)}) %reduce-scatter.3.cloned.1.call-update) | async-done | bytes 851984 | tf_op jit(solution)/shard_map/reduce_scatter | solution.py:211
  240.1 2.0 convert_element_type.29
  242.1 0.0 all-gather.6.cloned.1.call-update
  242.1 0.2 reduce-scatter.5.cloned.1.call-start
  242.3 38.8 %all-gather.6.cloned.1.call-done = bf16[256,6656]{1,0:T(8,128)(2,1)} async-done(((bf16[32,6656]{1,0:T(8,128)(2,1)}), bf16[256,6656]{1,0:T(8,128)(2,1)}) %all-gather.6.cloned.1.call-update) | async-done | bytes 3407888 | tf_op jit(solution)/shard_map/all_gather | solution.py:206
  281.1 10.6 %fusion.2.p_ref = f32[1536,256]{1,0:T(8,128)S(1)} fusion(bf16[1536,6656]{1,0:T(8,128)(2,1)} %add_convert_fusion, bf16[256,6656]{1,0:T(8,128)(2,1)} %all-gather.6.cloned.1.call-done), kind=kOutput, calls=%fused_computation.7 | convolution fusion | flops 5234491392 | bytes 25427968 | tf_op jit(solution)/shard_map/dot_general | solution.py:204
  291.8 90.3 %shard_map.59 = (f32[384,256]{1,0:T(8,128)S(1)}, bf16[1536,256]{1,0:T(8,128)(2,1)S(1)}) custom-call(f32[1536,256]{1,0:T(8,128)S(1)} %fusion.2.p_ref), custom_call_target="tpu_custom_call" | custom-call | tf_op jit(solution)/shard_map/pallas_call | solution.py:167
  382.1 14.7 %fusion.3 = f32[256,6656]{1,0:T(8,128)} fusion(bf16[1536,256]{1,0:T(8,128)(2,1)S(1)} %get-tuple-element.7, bf16[1536,6656]{1,0:T(8,128)(2,1)} %add_convert_fusion), kind=kOutput, calls=%fused_computation.8 | convolution fusion | flops 5234491392 | bytes 28049408 | tf_op jit(solution)/shard_map/dot_general | solution.py:212
  396.8 0.0 reduce-scatter.5.cloned.1.call-update
  396.8 0.0 all-gather.8.cloned.1.call-start
  396.8 75.9 %reduce-scatter.5.cloned.1.call-done = f32[32,6656]{1,0:T(8,128)} async-done(((f32[256,6656]{1,0:T(8,128)}), f32[32,6656]{1,0:T(8,128)}) %reduce-scatter.5.cloned.1.call-update) | async-done | bytes 851984 | tf_op jit(solution)/shard_map/reduce_scatter | solution.py:211
  472.7 1.3 multiply_reduce_fusion
  474.1 9.8 %psum.7 = f32[32]{0:T(128)S(1)} all-reduce(f32[32]{0:T(128)S(1)} %multiply_reduce_fusion), channel_id=1, replica_groups=mesh['row'=8,'col'=4] {'col'}, use_global_device_ids=true, to_apply=%region_3.0 | all-reduce | flops 32 | bytes 256 | tf_op jit(solution)/shard_map/psum | solution.py:218
  483.9 2.7 broadcast_divide_fusion
  486.5 0.0 all-gather.8.cloned.1.call-update
  486.6 37.1 %all-gather.8.cloned.1.call-done = bf16[256,6656]{1,0:T(8,128)(2,1)} async-done(((bf16[32,6656]{1,0:T(8,128)(2,1)}), bf16[256,6656]{1,0:T(8,128)(2,1)}) %all-gather.8.cloned.1.call-update) | async-done | bytes 3407888 | tf_op jit(solution)/shard_map/all_gather | solution.py:219
  523.7 18.3 %subtract_convert_fusion = bf16[1536,6656]{1,0:T(8,128)(2,1)} fusion(bf16[1536,6656]{1,0:T(8,128)(2,1)} %add_convert_fusion, bf16[1536,256]{1,0:T(8,128)(2,1)S(1)} %get-tuple-element.7, bf16[256,6656]{1,0:T(8,128)(2,1)} %all-gather.8.cloned.1.call-done), kind=kOutput, calls=%fused_computation | convolution fusion | flops 5275385856 | bytes 45088768 | tf_op jit(solution)/shard_map/dot_general | solution.py:221
  542.0 0.7 copy.7
  (1 shorter events, 0.0 us)
Async XLA Ops:
  7.2 46.2 %all-gather.4.cloned.1.call-start = ((), (), s32[]{:S(2)}) async-start(), calls=%async_computation.2 | async-start | bytes 3833856 | tf_op jit(solution)/shard_map/all_gather | solution.py:206
  9.2 230.9 %reduce-scatter.3.cloned.1.call-start = ((), (), s32[]{:S(2)}) async-start(), calls=%async_computation.3 | async-start | bytes 7667712 | tf_op jit(solution)/shard_map/reduce_scatter | solution.py:211
  53.4 103.1 %copy-start = (bf16[1536,6656]{1,0:T(8,128)(2,1)S(1)}, bf16[1536,6656]{1,0:T(8,128)(2,1)}, u32[]{:S(2)}) copy-start(bf16[1536,6656]{1,0:T(8,128)(2,1)} %add_convert_fusion) | copy-start | bytes 61341700
  164.2 117.0 %all-gather.6.cloned.1.call-start = ((), (), s32[]{:S(2)}) async-start(), calls=%async_computation.4 | async-start | bytes 3833856 | tf_op jit(solution)/shard_map/all_gather | solution.py:206
  242.1 230.7 %reduce-scatter.5.cloned.1.call-start = ((), (), s32[]{:S(2)}) async-start(), calls=%async_computation.5 | async-start | bytes 7667712 | tf_op jit(solution)/shard_map/reduce_scatter | solution.py:211
  396.8 126.9 %all-gather.8.cloned.1.call-start = ((), (), s32[]{:S(2)}) async-start(), calls=%async_computation.6 | async-start | bytes 3833856 | tf_op jit(solution)/shard_map/all_gather | solution.py:219
Sparse Core Ops, SparseCore 0:
  10.2 43.1 all-gather.3
  164.3 75.7 reduce-scatter.2
  242.3 38.7 all-gather.5
  396.9 75.7 reduce-scatter.4
  486.7 36.9 all-gather.7

commit v2 on v1

--- a/solution.py
+++ b/solution.py
@@ -10,7 +10,7 @@
 COLS = 26624
 POWER = 2
 BLOCK = 128
-PANEL = 8
+PANEL = 16
 MESH = pl.DeviceIdType.MESH
 HIGHEST = lax.Precision.HIGHEST
 
@@ -197,28 +197,227 @@
     return left, lax.all_gather(left.astype(jnp.bfloat16), "col", axis=0, tiled=True)
 
 
+def ring_kernel(n_row, part_ref, own_ref, whole_ref, peer_part, out_r, in_r, out_l, in_l,
+                xs, xr, rs, rr, ls, lr, gs, gr_, hs, hr, cs, cr):
+    row, col = lax.axis_index("row"), lax.axis_index("col")
+    chips = n_row // 2
+    last = chips - 1
+    z, core = lax.div(row, 2), lax.rem(row, 2)
+    peer = (z * 2 + 1 - core, col)
+    right = (lax.rem(row + 2, n_row), col)
+    left = (lax.rem(row + n_row - 2, n_row), col)
+    has_right, has_left = z < last, z > 0
+    columns = own_ref.shape[1]
+    width = 512 if columns % 512 == 0 else 128
+
+    barrier = pltpu.get_barrier_semaphore()
+    pl.semaphore_signal(barrier, inc=1, device_id=peer, device_id_type=MESH)
+
+    @pl.when(has_right)
+    def _():
+        pl.semaphore_signal(barrier, inc=1, device_id=right, device_id_type=MESH)
+
+    @pl.when(has_left)
+    def _():
+        pl.semaphore_signal(barrier, inc=1, device_id=left, device_id_type=MESH)
+
+    pl.semaphore_wait(barrier, 1 + has_right.astype(jnp.int32) + has_left.astype(jnp.int32))
+
+    def remote(src, dst, send, recv, device):
+        return pltpu.make_async_remote_copy(
+            src_ref=src, dst_ref=dst, send_sem=send, recv_sem=recv,
+            device_id=device, device_id_type=MESH,
+        )
+
+    def over_columns(body):
+        def step(i, carry):
+            body(pl.ds(pl.multiple_of(i * width, width), width))
+            return carry
+
+        lax.fori_loop(0, columns // width, step, 0)
+
+    def exchange(t):
+        return remote(part_ref.at[t, 1 - core], peer_part.at[t], xs.at[t], xr.at[t], peer)
+
+    order = []
+    for k in range(chips):
+        for t in (last - k, k):
+            if t not in order:
+                order.append(t)
+    for t in order:
+        exchange(t).start()
+
+    def chip_sum(t, at):
+        return part_ref[t, core, :, at] + peer_part[t, :, at]
+
+    def to_right(k):
+        return remote(out_r.at[k], in_r.at[k], rs.at[k], rr.at[k], right)
+
+    def to_left(k):
+        return remote(out_l.at[k], in_l.at[k], ls.at[k], lr.at[k], left)
+
+    arrived = []
+    for k in range(last):
+        for t, rightward in ((last - k, True), (k, False)):
+            if t not in arrived:
+                arrived.append(t)
+                exchange(t).wait_recv()
+            out, into = (out_r, in_r) if rightward else (out_l, in_l)
+            copy = to_right(k) if rightward else to_left(k)
+            first = z == (0 if rightward else last)
+            before = z < t if rightward else z > t
+            reached = z <= t if rightward else z >= t
+
+            @pl.when(jnp.logical_and(jnp.logical_not(first), reached))
+            def _():
+                copy.wait_recv()
+
+            @pl.when(jnp.logical_and(first, before))
+            def _():
+                def body(at):
+                    out[k, :, at] = chip_sum(t, at).astype(jnp.bfloat16)
+
+                over_columns(body)
+
+            @pl.when(jnp.logical_and(jnp.logical_not(first), before))
+            def _():
+                def body(at):
+                    out[k, :, at] = (chip_sum(t, at) + into[k, :, at].astype(jnp.float32)).astype(jnp.bfloat16)
+
+                over_columns(body)
+
+            @pl.when(before)
+            def _():
+                copy.start()
+
+    for t in range(chips):
+        if t not in arrived:
+            exchange(t).wait_recv()
+    for t in range(chips):
+        @pl.when(z == t)
+        def _():
+            def body(at):
+                total = chip_sum(t, at)
+                if t > 0:
+                    total = total + in_r[last - t, :, at].astype(jnp.float32)
+                if t < last:
+                    total = total + in_l[t, :, at].astype(jnp.float32)
+                own_ref[:, at] = total
+                whole_ref[t, core, :, at] = total.astype(jnp.bfloat16)
+
+            over_columns(body)
+
+    def same_place(j, send, recv, device):
+        place = whole_ref.at[j, core]
+        return remote(place, place, send, recv, device)
+
+    def from_peer(j, send, recv):
+        place = whole_ref.at[j, 1 - core]
+        return remote(place, place, send, recv, peer)
+
+    same_place(z, cs.at[0], cr.at[0], peer).start()
+    for k in range(last):
+        @pl.when(jnp.logical_and(has_right, z - k >= 0))
+        def _():
+            same_place(z - k, gs.at[k], gr_.at[k], right).start()
+
+        @pl.when(jnp.logical_and(has_left, z + k <= last))
+        def _():
+            same_place(z + k, hs.at[k], hr.at[k], left).start()
+
+        @pl.when(z - 1 - k >= 0)
+        def _():
+            same_place(z - 1 - k, gs.at[k], gr_.at[k], right).wait_recv()
+            same_place(z - 1 - k, cs.at[1 + k], cr.at[1 + k], peer).start()
+
+        @pl.when(z + 1 + k <= last)
+        def _():
+            same_place(z + 1 + k, hs.at[k], hr.at[k], left).wait_recv()
+            same_place(z + 1 + k, cs.at[chips + k], cr.at[chips + k], peer).start()
+
+    from_peer(z, cs.at[0], cr.at[0]).wait_recv()
+    same_place(z, cs.at[0], cr.at[0], peer).wait_send()
+    for t in order:
+        exchange(t).wait_send()
+    for k in range(last):
+        @pl.when(z < last - k)
+        def _():
+            to_right(k).wait_send()
+
+        @pl.when(z > k)
+        def _():
+            to_left(k).wait_send()
+
+        @pl.when(jnp.logical_and(has_right, z - k >= 0))
+        def _():
+            same_place(z - k, gs.at[k], gr_.at[k], right).wait_send()
+
+        @pl.when(jnp.logical_and(has_left, z + k <= last))
+        def _():
+            same_place(z + k, hs.at[k], hr.at[k], left).wait_send()
+
+        @pl.when(z - 1 - k >= 0)
+        def _():
+            same_place(z - 1 - k, cs.at[1 + k], cr.at[1 + k], peer).wait_send()
+            from_peer(z - 1 - k, cs.at[1 + k], cr.at[1 + k]).wait_recv()
+
+        @pl.when(z + 1 + k <= last)
+        def _():
+            same_place(z + 1 + k, cs.at[chips + k], cr.at[chips + k], peer).wait_send()
+            from_peer(z + 1 + k, cs.at[chips + k], cr.at[chips + k]).wait_recv()
+
+
+def right_of(partial, n_row):
+    rank, columns = partial.shape
+    gr = rank // n_row
+    if gr % 16 != 0:
+        own = lax.psum_scatter(partial, "row", scatter_dimension=0, tiled=True)
+        return own, lax.all_gather(own.astype(jnp.bfloat16), "row", axis=0, tiled=True)
+    chips = n_row // 2
+    hops = chips - 1
+    vmem = pl.BlockSpec(memory_space=pltpu.VMEM)
+    dma = pltpu.SemaphoreType.DMA
+    wire = pltpu.VMEM((hops, gr, columns), jnp.bfloat16)
+    own, whole = pl.pallas_call(
+        functools.partial(ring_kernel, n_row),
+        out_shape=[
+            jax.ShapeDtypeStruct((gr, columns), jnp.float32),
+            jax.ShapeDtypeStruct((chips, 2, gr, columns), jnp.bfloat16),
+        ],
+        in_specs=[vmem],
+        out_specs=[vmem, vmem],
+        scratch_shapes=[
+            pltpu.VMEM((chips, gr, columns), jnp.float32),
+            wire, wire, wire, wire,
+            dma((chips,)), dma((chips,)),
+            dma((hops,)), dma((hops,)), dma((hops,)), dma((hops,)),
+            dma((hops,)), dma((hops,)), dma((hops,)), dma((hops,)),
+            dma((2 * chips - 1,)), dma((2 * chips - 1,)),
+        ],
+        compiler_params=pltpu.CompilerParams(
+            collective_id=1, has_side_effects=True, vmem_limit_bytes=40 * 1024 * 1024
+        ),
+    )(partial.reshape(chips, 2, gr, columns))
+    return own, whole.reshape(rank, columns)
+
+
 def per_device(n_row, n_col, momentum, gradient, basis):
     buffer = (momentum.astype(jnp.float32) + gradient.astype(jnp.float32)).astype(jnp.bfloat16)
-    directions = basis.astype(jnp.bfloat16)
+    whole = lax.all_gather(basis.astype(jnp.bfloat16), "row", axis=0, tiled=True)
     for step in range(POWER):
         partial_value = lax.dot_general(
-            buffer,
-            lax.all_gather(directions, "row", axis=0, tiled=True),
-            (((1,), (1,)), ((), ())),
-            preferred_element_type=jnp.float32,
+            buffer, whole, (((1,), (1,)), ((), ())), preferred_element_type=jnp.float32
         )
         left_share, left_half = left_of(partial_value, n_row, n_col)
-        right_own = lax.psum_scatter(
+        right_own, whole = right_of(
             lax.dot_general(
                 left_half, buffer, (((0,), (0,)), ((), ())), preferred_element_type=jnp.float32
             ),
-            "row", scatter_dimension=0, tiled=True,
+            n_row,
         )
-        directions = right_own.astype(jnp.bfloat16)
     squares = lax.psum(jnp.sum(right_own * right_own, axis=1), "col")
-    right_whole = lax.all_gather(directions, "row", axis=0, tiled=True)
     basis_new = right_own / jnp.sqrt(squares[:, None] / COLS + epsilon)
-    update = jnp.dot(left_half, right_whole, preferred_element_type=jnp.float32)
+    update = jnp.dot(left_half, whole, preferred_element_type=jnp.float32)
     momentum_new = (buffer.astype(jnp.float32) - (1.0 - decay_rate) * update).astype(jnp.bfloat16)
     return (momentum_new, basis_new, left_share)
 

time: 550 us -> 539 us (0.980)
  Pallas kernels: 181 us -> 411 us
  waiting for transfers between devices: 250 us -> 21.8 us
  matrix products: 63.3 us -> 57.8 us
    pallas_call x0 -> x2, Pallas kernels: none -> 239 us  [right_of(): pl.pallas_call(functools.partial(ring_kernel, n_row), out_shape=[jax.Shap...]
    reduce_scatter x2 -> x0, waiting for transfers between devices: 152 us -> none  [per_device(): lax.psum_scatter(lax.dot_general(left_half, buffer, (((0,), (0,)), ((), (...]
    all_gather x3 -> x1, waiting for transfers between devices: 97.7 us -> 21.8 us  [per_device(): lax.all_gather(basis.astype(jnp.bfloat16), 'row', axis=0, tiled=True)]
    pallas_call x2, Pallas kernels: 181 us -> 172 us  [left_of(): pl.pallas_call(functools.partial(left_kernel, n_row, n_col, gather), out_...]
  transfers between devices with their start and end apart: 5 -> 1, of which waited for: 5 -> 1; matrix products, arithmetic and copies ran while one was open for 4% -> 4% of each run, Pallas kernels for 0% -> 0%
where the time goes in v2:
time: 539 us
  Pallas kernels  411 us (76%)
  matrix products  57.8 us (11%)
  other arithmetic  25.6 us (5%)
  waiting for transfers between devices  21.8 us (4%)
  between operations  14.1 us (3%)
  blocking collectives  8.66 us (2%)
    pallas_call x2, Pallas kernels, right_of(): pl.pallas_call(functools.partial(ring_kernel, n_row), out_shape=[jax.Shap...  239 us
    pallas_call x2, Pallas kernels, left_of(): pl.pallas_call(functools.partial(left_kernel, n_row, n_col, gather), out_...  172 us
    convert_element_type x1, other arithmetic, per_device(): (momentum.astype(jnp.float32) + gradient.astype(jnp.float32)).astype(jnp....  22.4 us
    all_gather x1, waiting for transfers between devices, per_device(): lax.all_gather(basis.astype(jnp.bfloat16), 'row', axis=0, tiled=True)  21.8 us
    dot_general x2, matrix products, per_device(): lax.dot_general(buffer, whole, (((1,), (1,)), ((), ())), preferred_elemen...  20.3 us
    dot_general x2, matrix products, per_device(): lax.dot_general(left_half, buffer, (((0,), (0,)), ((), ())), preferred_el...  19.8 us
    dot_general x1, matrix products, per_device(): update = jnp.dot(left_half, whole, preferred_element_type=jnp.float32)  17.7 us
  transfers between devices with their start and end apart: 1, of which 1 were waited for; matrix products, arithmetic and copies ran while one was open for 4% of the time, Pallas kernels for 0%

profile of v2, /device:TPU:0, one launch (start us, length us, event | category | flops | bytes accessed | tf_op | source)
XLA Modules:
  0.0 539.3 jit_solution(5379774791013057643)
XLA Ops:
  7.2 0.0 all-gather.2.cloned.1.call-start
  7.2 2.0 convert_element_type.22
  9.2 0.0 all-gather.2.cloned.1.call-update
  9.2 22.4 %add_convert_fusion = bf16[1536,6656]{1,0:T(8,128)(2,1)} fusion(bf16[1536,6656]{1,0:T(8,128)(2,1)} %param.4, bf16[1536,6656]{1,0:T(8,128)(2,1)} %param.3), kind=kLoop, calls=%fused_computation.1 | loop fusion | flops 40894464 | bytes 61341696 | tf_op jit(solution)/shard_map/convert_element_type | solution.py:405
  31.6 21.8 %all-gather.2.cloned.1.call-done = bf16[256,6656]{1,0:T(8,128)(2,1)} async-done(((bf16[32,6656]{1,0:T(8,128)(2,1)}), bf16[256,6656]{1,0:T(8,128)(2,1)}) %all-gather.2.cloned.1.call-update) | async-done | bytes 3407888 | tf_op jit(solution)/shard_map/all_gather | solution.py:406
  53.4 10.6 %fusion.p_ref = f32[1536,256]{1,0:T(8,128)S(1)} fusion(bf16[1536,6656]{1,0:T(8,128)(2,1)} %add_convert_fusion, bf16[256,6656]{1,0:T(8,128)(2,1)} %all-gather.2.cloned.1.call-done), kind=kOutput, calls=%fused_computation.5 | convolution fusion | flops 5234491392 | bytes 25427968 | tf_op jit(solution)/shard_map/dot_general | solution.py:408
  64.0 86.5 %shard_map.58 = (f32[384,256]{1,0:T(8,128)}, bf16[1536,256]{1,0:T(8,128)(2,1)S(1)}) custom-call(f32[1536,256]{1,0:T(8,128)S(1)} %fusion.p_ref), custom_call_target="tpu_custom_call" | custom-call | tf_op jit(solution)/shard_map/pallas_call | solution.py:167
  150.6 9.9 %fusion.1 = f32[256,6656]{1,0:T(8,128)S(1)} fusion(bf16[1536,256]{1,0:T(8,128)(2,1)S(1)} %get-tuple-element.9, bf16[1536,6656]{1,0:T(8,128)(2,1)} %add_convert_fusion), kind=kOutput, calls=%fused_computation.6 | convolution fusion | flops 5234491392 | bytes 28049408 | tf_op jit(solution)/shard_map/dot_general | solution.py:413
  160.4 119.7 %shard_map.59 = (f32[32,6656]{1,0:T(8,128)}, bf16[4,2,32,6656]{3,2,1,0:T(8,128)(2,1)S(1)}) custom-call(f32[4,2,32,6656]{3,2,1,0:T(8,128)S(1)} %bitcast.14), custom_call_target="tpu_custom_call" | custom-call | tf_op jit(solution)/shard_map/pallas_call | solution.py:381
  280.1 9.7 %fusion.2.p_ref = f32[1536,256]{1,0:T(8,128)S(1)} fusion(bf16[1536,6656]{1,0:T(8,128)(2,1)} %add_convert_fusion, bf16[256,6656]{1,0:T(8,128)(2,1)S(1)} %bitcast.17), kind=kOutput, calls=%fused_computation.7 | convolution fusion | flops 5234491392 | bytes 25427968 | tf_op jit(solution)/shard_map/dot_general | solution.py:408
  289.8 85.2 %shard_map.60 = (f32[384,256]{1,0:T(8,128)S(1)}, bf16[1536,256]{1,0:T(8,128)(2,1)S(1)}) custom-call(f32[1536,256]{1,0:T(8,128)S(1)} %fusion.2.p_ref), custom_call_target="tpu_custom_call" | custom-call | tf_op jit(solution)/shard_map/pallas_call | solution.py:167
  375.1 9.9 %fusion.3 = f32[256,6656]{1,0:T(8,128)S(1)} fusion(bf16[1536,256]{1,0:T(8,128)(2,1)S(1)} %get-tuple-element.11, bf16[1536,6656]{1,0:T(8,128)(2,1)} %add_convert_fusion), kind=kOutput, calls=%fused_computation.8 | convolution fusion | flops 5234491392 | bytes 28049408 | tf_op jit(solution)/shard_map/dot_general | solution.py:413
  385.0 119.1 %shard_map.61 = (f32[32,6656]{1,0:T(8,128)S(1)}, bf16[4,2,32,6656]{3,2,1,0:T(8,128)(2,1)S(1)}) custom-call(f32[4,2,32,6656]{3,2,1,0:T(8,128)S(1)} %bitcast.15), custom_call_target="tpu_custom_call" | custom-call | tf_op jit(solution)/shard_map/pallas_call | solution.py:381
  504.1 17.7 %subtract_convert_fusion = bf16[1536,6656]{1,0:T(8,128)(2,1)} fusion(bf16[1536,6656]{1,0:T(8,128)(2,1)} %add_convert_fusion, bf16[1536,256]{1,0:T(8,128)(2,1)S(1)} %get-tuple-element.11, bf16[256,6656]{1,0:T(8,128)(2,1)S(1)} %bitcast.16), kind=kOutput, calls=%fused_computation | convolution fusion | flops 5275385856 | bytes 45088768 | tf_op jit(solution)/shard_map/dot_general | solution.py:420
  521.8 0.2 multiply_reduce_fusion
  522.0 8.7 %psum.7 = f32[32]{0:T(128)S(1)} all-reduce(f32[32]{0:T(128)S(1)} %multiply_reduce_fusion), channel_id=1, replica_groups=mesh['row'=8,'col'=4] {'col'}, use_global_device_ids=true, to_apply=%region_1.0 | all-reduce | flops 32 | bytes 256 | tf_op jit(solution)/shard_map/psum | solution.py:418
  530.6 1.0 broadcast_divide_fusion
  531.7 0.7 copy.7
  (1 shorter events, 0.0 us)
Async XLA Ops:
  7.2 46.2 %all-gather.2.cloned.1.call-start = ((), (), s32[]{:S(2)}) async-start(), calls=%async_computation | async-start | bytes 3833856 | tf_op jit(solution)/shard_map/all_gather | solution.py:406
Sparse Core Ops, SparseCore 0:
  10.2 43.1 all-gather.1

commit v3 on v2

--- a/solution.py
+++ b/solution.py
@@ -256,39 +256,46 @@
     def to_left(k):
         return remote(out_l.at[k], in_l.at[k], ls.at[k], lr.at[k], left)
 
+    def hop(k, t, rightward, turn):
+        out, into = (out_r, in_r) if rightward else (out_l, in_l)
+        copy = to_right(k) if rightward else to_left(k)
+        first = z == (0 if rightward else last)
+        before = jnp.logical_and(turn, z < t if rightward else z > t)
+        reached = jnp.logical_and(turn, z <= t if rightward else z >= t)
+
+        @pl.when(jnp.logical_and(jnp.logical_not(first), reached))
+        def _():
+            copy.wait_recv()
+
+        @pl.when(jnp.logical_and(first, before))
+        def _():
+            def body(at):
+                out[k, :, at] = chip_sum(t, at).astype(jnp.bfloat16)
+
+            over_columns(body)
+
+        @pl.when(jnp.logical_and(jnp.logical_not(first), before))
+        def _():
+            def body(at):
+                out[k, :, at] = (chip_sum(t, at) + into[k, :, at].astype(jnp.float32)).astype(jnp.bfloat16)
+
+            over_columns(body)
+
+        @pl.when(before)
+        def _():
+            copy.start()
+
+    lower = z < chips // 2
+    upper = jnp.logical_not(lower)
     arrived = []
     for k in range(last):
-        for t, rightward in ((last - k, True), (k, False)):
+        for t in (last - k, k):
             if t not in arrived:
                 arrived.append(t)
                 exchange(t).wait_recv()
-            out, into = (out_r, in_r) if rightward else (out_l, in_l)
-            copy = to_right(k) if rightward else to_left(k)
-            first = z == (0 if rightward else last)
-            before = z < t if rightward else z > t
-            reached = z <= t if rightward else z >= t
-
-            @pl.when(jnp.logical_and(jnp.logical_not(first), reached))
-            def _():
-                copy.wait_recv()
-
-            @pl.when(jnp.logical_and(first, before))
-            def _():
-                def body(at):
-                    out[k, :, at] = chip_sum(t, at).astype(jnp.bfloat16)
-
-                over_columns(body)
-
-            @pl.when(jnp.logical_and(jnp.logical_not(first), before))
-            def _():
-                def body(at):
-                    out[k, :, at] = (chip_sum(t, at) + into[k, :, at].astype(jnp.float32)).astype(jnp.bfloat16)
-
-                over_columns(body)
-
-            @pl.when(before)
-            def _():
-                copy.start()
+        hop(k, last - k, True, lower)
+        hop(k, k, False, z >= 0)
+        hop(k, last - k, True, upper)
 
     for t in range(chips):
         if t not in arrived:

time: 539 us -> 477 us (0.88)
  Pallas kernels: 411 us -> 346 us
    pallas_call x2, Pallas kernels: 239 us -> 173 us  [right_of(): pl.pallas_call(functools.partial(ring_kernel, n_row), out_shape=[jax.Shap...]
  transfers between devices with their start and end apart: 1 -> 1, of which waited for: 1 -> 1; matrix products, arithmetic and copies ran while one was open for 4% -> 5% of each run, Pallas kernels for 0% -> 0%
where the time goes in v3:
time: 477 us
  Pallas kernels  346 us (73%)
  matrix products  57.8 us (12%)
  other arithmetic  25.6 us (5%)
  waiting for transfers between devices  21.8 us (5%)
  between operations  14.1 us (3%)
  blocking collectives  10.7 us (2%)
    pallas_call x2, Pallas kernels, right_of(): pl.pallas_call(functools.partial(ring_kernel, n_row), out_shape=[jax.Shap...  173 us
    pallas_call x2, Pallas kernels, left_of(): pl.pallas_call(functools.partial(left_kernel, n_row, n_col, gather), out_...  173 us
    convert_element_type x1, other arithmetic, per_device(): (momentum.astype(jnp.float32) + gradient.astype(jnp.float32)).astype(jnp....  22.4 us
    all_gather x1, waiting for transfers between devices, per_device(): lax.all_gather(basis.astype(jnp.bfloat16), 'row', axis=0, tiled=True)  21.8 us
    dot_general x2, matrix products, per_device(): lax.dot_general(buffer, whole, (((1,), (1,)), ((), ())), preferred_elemen...  20.3 us
    dot_general x2, matrix products, per_device(): lax.dot_general(left_half, buffer, (((0,), (0,)), ((), ())), preferred_el...  19.8 us
    dot_general x1, matrix products, per_device(): update = jnp.dot(left_half, whole, preferred_element_type=jnp.float32)  17.7 us
    psum x1, blocking collectives, per_device(): squares = lax.psum(jnp.sum(right_own * right_own, axis=1), 'col')  10.7 us
  transfers between devices with their start and end apart: 1, of which 1 were waited for; matrix products, arithmetic and copies ran while one was open for 5% of the time, Pallas kernels for 0%

profile of v3, /device:TPU:0, one launch (start us, length us, event | category | flops | bytes accessed | tf_op | source)
XLA Modules:
  0.0 477.1 jit_solution(1210685109434073136)
XLA Ops:
  7.2 0.0 all-gather.2.cloned.1.call-start
  7.2 2.0 convert_element_type.22
  9.2 0.0 all-gather.2.cloned.1.call-update
  9.2 22.4 %add_convert_fusion = bf16[1536,6656]{1,0:T(8,128)(2,1)} fusion(bf16[1536,6656]{1,0:T(8,128)(2,1)} %param.4, bf16[1536,6656]{1,0:T(8,128)(2,1)} %param.3), kind=kLoop, calls=%fused_computation.1 | loop fusion | flops 40894464 | bytes 61341696 | tf_op jit(solution)/shard_map/convert_element_type | solution.py:412
  31.6 21.8 %all-gather.2.cloned.1.call-done = bf16[256,6656]{1,0:T(8,128)(2,1)} async-done(((bf16[32,6656]{1,0:T(8,128)(2,1)}), bf16[256,6656]{1,0:T(8,128)(2,1)}) %all-gather.2.cloned.1.call-update) | async-done | bytes 3407888 | tf_op jit(solution)/shard_map/all_gather | solution.py:413
  53.4 10.6 %fusion.p_ref = f32[1536,256]{1,0:T(8,128)S(1)} fusion(bf16[1536,6656]{1,0:T(8,128)(2,1)} %add_convert_fusion, bf16[256,6656]{1,0:T(8,128)(2,1)} %all-gather.2.cloned.1.call-done), kind=kOutput, calls=%fused_computation.5 | convolution fusion | flops 5234491392 | bytes 25427968 | tf_op jit(solution)/shard_map/dot_general | solution.py:415
  64.0 86.5 %shard_map.58 = (f32[384,256]{1,0:T(8,128)}, bf16[1536,256]{1,0:T(8,128)(2,1)S(1)}) custom-call(f32[1536,256]{1,0:T(8,128)S(1)} %fusion.p_ref), custom_call_target="tpu_custom_call" | custom-call | tf_op jit(solution)/shard_map/pallas_call | solution.py:167
  150.6 9.9 %fusion.1 = f32[256,6656]{1,0:T(8,128)S(1)} fusion(bf16[1536,256]{1,0:T(8,128)(2,1)S(1)} %get-tuple-element.9, bf16[1536,6656]{1,0:T(8,128)(2,1)} %add_convert_fusion), kind=kOutput, calls=%fused_computation.6 | convolution fusion | flops 5234491392 | bytes 28049408 | tf_op jit(solution)/shard_map/dot_general | solution.py:420
  160.4 87.4 %shard_map.59 = (f32[32,6656]{1,0:T(8,128)}, bf16[4,2,32,6656]{3,2,1,0:T(8,128)(2,1)S(1)}) custom-call(f32[4,2,32,6656]{3,2,1,0:T(8,128)S(1)} %bitcast.14), custom_call_target="tpu_custom_call" | custom-call | tf_op jit(solution)/shard_map/pallas_call | solution.py:388
  247.9 9.7 %fusion.2.p_ref = f32[1536,256]{1,0:T(8,128)S(1)} fusion(bf16[1536,6656]{1,0:T(8,128)(2,1)} %add_convert_fusion, bf16[256,6656]{1,0:T(8,128)(2,1)S(1)} %bitcast.17), kind=kOutput, calls=%fused_computation.7 | convolution fusion | flops 5234491392 | bytes 25427968 | tf_op jit(solution)/shard_map/dot_general | solution.py:415
  257.5 86.5 %shard_map.60 = (f32[384,256]{1,0:T(8,128)S(1)}, bf16[1536,256]{1,0:T(8,128)(2,1)S(1)}) custom-call(f32[1536,256]{1,0:T(8,128)S(1)} %fusion.2.p_ref), custom_call_target="tpu_custom_call" | custom-call | tf_op jit(solution)/shard_map/pallas_call | solution.py:167
  344.1 9.9 %fusion.3 = f32[256,6656]{1,0:T(8,128)S(1)} fusion(bf16[1536,256]{1,0:T(8,128)(2,1)S(1)} %get-tuple-element.11, bf16[1536,6656]{1,0:T(8,128)(2,1)} %add_convert_fusion), kind=kOutput, calls=%fused_computation.8 | convolution fusion | flops 5234491392 | bytes 28049408 | tf_op jit(solution)/shard_map/dot_general | solution.py:420
  354.0 85.9 %shard_map.61 = (f32[32,6656]{1,0:T(8,128)S(1)}, bf16[4,2,32,6656]{3,2,1,0:T(8,128)(2,1)S(1)}) custom-call(f32[4,2,32,6656]{3,2,1,0:T(8,128)S(1)} %bitcast.15), custom_call_target="tpu_custom_call" | custom-call | tf_op jit(solution)/shard_map/pallas_call | solution.py:388
  439.9 17.7 %subtract_convert_fusion = bf16[1536,6656]{1,0:T(8,128)(2,1)} fusion(bf16[1536,6656]{1,0:T(8,128)(2,1)} %add_convert_fusion, bf16[1536,256]{1,0:T(8,128)(2,1)S(1)} %get-tuple-element.11, bf16[256,6656]{1,0:T(8,128)(2,1)S(1)} %bitcast.16), kind=kOutput, calls=%fused_computation | convolution fusion | flops 5275385856 | bytes 45088768 | tf_op jit(solution)/shard_map/dot_general | solution.py:427
  457.6 0.2 multiply_reduce_fusion
  457.8 10.7 %psum.7 = f32[32]{0:T(128)S(1)} all-reduce(f32[32]{0:T(128)S(1)} %multiply_reduce_fusion), channel_id=1, replica_groups=mesh['row'=8,'col'=4] {'col'}, use_global_device_ids=true, to_apply=%region_1.0 | all-reduce | flops 32 | bytes 256 | tf_op jit(solution)/shard_map/psum | solution.py:425
  468.5 1.0 broadcast_divide_fusion
  469.5 0.7 copy.7
  (1 shorter events, 0.0 us)
Async XLA Ops:
  7.2 46.2 %all-gather.2.cloned.1.call-start = ((), (), s32[]{:S(2)}) async-start(), calls=%async_computation | async-start | bytes 3833856 | tf_op jit(solution)/shard_map/all_gather | solution.py:413
Sparse Core Ops, SparseCore 0:
  10.2 43.1 all-gather.1
